TPU v7x, 512 devices: a whole 4x8x8 slice. The times are simulated.
512 devices in a mesh: tm: 16 (over x, z_hi, core), cell: 32 (over y, z_lo).
Axes of the slice: x: 4, y: 8, z: 8 (z_hi: 2, z_lo: 4; z = z_hi * 4 + z_lo), core: 2. Of those that a mesh axis runs over, the one named last changes fastest.
Arguments:
- sensitivity: bfloat16 [2048, 16, 16384], P(None, 'tm', 'cell'), may hold values from -0.25 to 0.25
- duals: bfloat16 [2048, 128], P(('tm', 'cell')), may hold values from -6 to 6
- time_cov: float32 [16, 16], replicated, may hold values from 0.05 to 0.5
- cell_coords: int32 [2, 16384], P(None, 'cell'), may hold values from 0 to 127, as said below
- obs_time: int32 [2048], replicated, may hold values from 0 to 15
- obs_owner: int32 [2048], replicated, may hold values from 0 to 2047, each once
Outputs:
- product: float32 [2048, 128], P(('tm', 'cell'))
Inputs may be any that keep to these rules, and one draw needn't show every extreme that they name: `cell_coords`: every cell has its own grid position; rows lie below 128 and columns below 128. `obs_owner`: every observation stands in exactly one slot.
All inputs are finite; a program needn't handle non-finite values.
Results may differ from a plain program's by a relative error of at most 0.0049.
Values may be sent and summed in bfloat16 or wider, within the bound.
No kernel may reach another device: no remote copies, remote signals or barrier semaphores. Data moves between devices by JAX's collectives and lax.ppermute only.
A program may use at most 64 MiB of HBM per device.

v0:
```python
import jax
import jax.numpy as jnp
from jax import lax
from jax.sharding import Mesh
from jax.sharding import PartitionSpec as P

LSCALE = 4
TM = ("tm_0", "tm_1", "tm_2")
TM_CELL = ("tm_0", "tm_1", "tm_2", "cell_0", "cell_1")
CELL = ("cell_0", "cell_1")


def laid_out(pieces, dim):
    pieces = jnp.moveaxis(pieces, 0, dim)
    shape = pieces.shape
    return pieces.reshape(*shape[:dim], shape[dim] * shape[dim + 1], *shape[dim + 2 :])


def sent_to_all(array, axis):
    copies = jnp.broadcast_to(array, (lax.axis_size(axis), *array.shape))
    return lax.all_to_all(copies, axis, split_axis=0, concat_axis=0, tiled=True)


def gathered_copies(array, axis, dim):
    return laid_out(sent_to_all(array, axis), dim)


def cut_along(array, dim, length):
    shape = array.shape
    pieces = array.reshape(*shape[:dim], length, shape[dim] // length, *shape[dim + 1 :])
    return jnp.moveaxis(pieces, dim, 0)


def edges_of(length, count):
    hop = length // count
    if hop >= 8:
        hop -= hop % 8
    return [hop * k for k in range(1, count)]


def own_block(pieces, axes, sequence):
    inside = pieces.shape[1:]
    pieces = pieces.reshape(*(lax.axis_size(a) for a in axes), *inside)
    pieces = jnp.moveaxis(pieces, sequence, range(len(axes))).reshape(-1, *inside)
    for k in sequence:
        pieces = lax.psum_scatter(pieces, axes[k], scatter_dimension=0, tiled=True)
    return pieces[0]


def sum_at_once(array, axes, dim):
    pieces = cut_along(array, dim, lax.axis_size(axes))
    widest = max(range(1, max(2, pieces.ndim - 1)), key=lambda d: pieces.shape[d])
    count, done = (len(axes), [])
    for first, slab in enumerate(
        jnp.split(pieces, edges_of(pieces.shape[widest], count), axis=widest)
    ):
        if slab.size:
            sequence = [(first + k) % count for k in range(count)]
            done.append(own_block(slab, axes, sequence))
    return jnp.concatenate(done, axis=widest - 1)


def covariance(left_coords, right_coords):
    row_gap = (left_coords[0][:, None] - right_coords[0][None, :]).astype(jnp.float32)
    col_gap = (left_coords[1][:, None] - right_coords[1][None, :]).astype(jnp.float32)
    distance = jnp.sqrt(row_gap * row_gap + col_gap * col_gap)
    return (jnp.exp(-distance / LSCALE) / (8.0 * LSCALE)).astype(jnp.bfloat16)


def per_device(sensitivity, duals, time_cov, cell_coords, obs_time, obs_owner):
    obs_count = sensitivity.shape[0]
    time_count = sensitivity.shape[1]
    cell_count = sensitivity.shape[2]
    real_count = duals.shape[1]
    first_time = lax.axis_index(TM) * time_count
    time_index = first_time + jnp.arange(time_count, dtype=jnp.int32)
    live = time_index[None, :, None] <= obs_time[:, None, None]
    masked = jnp.where(live, sensitivity, jnp.zeros((), jnp.bfloat16))
    flattened = masked.reshape(obs_count, time_count * cell_count)
    picked = flattened
    adjoint = lax.dot_general(
        picked,
        lax.all_gather(duals, TM_CELL, axis=0, tiled=True),
        (((0,), (0,)), ((), ())),
        preferred_element_type=jnp.float32,
    )
    local_adj = (
        adjoint.astype(jnp.bfloat16).reshape(time_count, cell_count, real_count).transpose(1, 0, 2)
    )
    all_coords = gathered_copies(cell_coords, CELL, 1)
    spread_adj = lax.all_to_all(local_adj, TM, split_axis=2, concat_axis=1, tiled=True)
    values = jnp.einsum(
        "st,ctr->csr", time_cov, spread_adj.astype(jnp.float32), precision=lax.Precision.HIGHEST
    ).astype(jnp.bfloat16)
    portion = lax.all_gather(values, CELL, axis=0, tiled=True)
    kernel = covariance(cell_coords, all_coords)
    summed = jnp.dot(
        kernel, portion.reshape(portion.shape[0], -1), preferred_element_type=jnp.float32
    )
    weighted = lax.all_to_all(
        summed.reshape(values.shape).astype(jnp.bfloat16),
        TM,
        split_axis=1,
        concat_axis=2,
        tiled=True,
    )
    weighted_flat = weighted.transpose(1, 0, 2).reshape(time_count * cell_count, real_count)
    picked = jnp.take(flattened, obs_owner, axis=0)
    return sum_at_once(
        jnp.dot(picked, weighted_flat, preferred_element_type=jnp.float32), TM_CELL, 0
    )


def solution(mesh):
    split = Mesh(mesh.devices.reshape(4, 2, 2, 8, 4), ("tm_0", "tm_1", "tm_2", "cell_0", "cell_1"))
    return jax.shard_map(
        per_device,
        mesh=split,
        in_specs=(P(None, TM, CELL), P(TM_CELL, None), P(), P(None, CELL), P(), P()),
        out_specs=P(TM_CELL, None),
        check_vma=False,
    )
```

profile of v0, /device:TPU:2, one launch (start us, length us, event | category | flops | bytes accessed | tf_op | source)
XLA Modules:
  0.0 1611.9 jit_solution(16433688849147574105)
XLA Ops:
  6.5 0.0 copy-start
  6.5 0.0 all-gather.3.cloned.1.call-start
  6.5 1138.5 %all-gather = bf16[512,4,128]{2,1,0:T(4,128)(2,1)S(1)} all-gather(bf16[1,4,128]{2,1,0:T(4,128)(2,1)} %bitcast.57), channel_id=1, replica_groups=mesh['tm_0'=4,'tm_1'=2,'tm_2'=2,'cell_0'=8,'cell_1'=4] {'tm_0','tm_1','t..., dimensions={0}, use_global_device_ids=true | all-gather | bytes 525312 | tf_op jit(solution)/shard_map/all_gather | solution.py:83
  1145.0 0.7 broadcast_compare_fusion
  1145.7 1.8 select_bitcast_fusion
  1147.5 0.8 fusion.14
  1148.3 0.2 copy.17
  1148.5 0.5 broadcast.41
  1149.0 1.4 reduce
  1150.4 0.1 reshape.87
  1150.5 126.0 %all_to_all.26 = bf16[16,2,2048]{2,1,0:T(2,128)(2,1)S(1)} all-to-all(bf16[16,2,2048]{2,1,0:T(2,128)(2,1)S(1)} %reshape.87), channel_id=1, replica_groups=mesh['tm_0'=4,'tm_1'=2,'tm_2'=2,'cell_0'=8,'cell_1'=4] {'tm_0','tm_1','t..., dimensions={0} | all-to-all | bytes 262144 | tf_op jit(solution)/shard_map/all_to_all | solution.py:91
  1276.5 0.1 reshape.88
  1276.6 0.0 copy-done
  1276.7 0.9 fusion.15
  1277.6 0.0 all-gather.3.cloned.1.call-update
  1277.6 0.0 copy-done.3
  1277.6 0.7 broadcast_in_dim.33
  1278.3 3.9 all-to-all-start
  1282.2 0.0 copy-done.2
  1282.2 9.2 gather_fusion
  1291.4 3.9 all-to-all-done
  1295.3 0.1 fusion.22
  1295.4 136.2 %all-gather.3.cloned.1.call-done = bf16[16384,16,8]{0,1,2:T(8,128)(2,1)} async-done(((bf16[512,16,8]{0,1,2:T(8,128)(2,1)}), bf16[16384,16,8]{0,1,2:T(8,128)(2,1)}) %all-gather.3.cloned.1.call-update) | async-done | bytes 4194320 | tf_op jit(solution)/shard_map/all_gather | solution.py:95
  1431.6 22.9 %fusion.9 = bf16[512,16,8]{0,1,2:T(8,128)(2,1)S(1)} fusion(bf16[16384,16,8]{0,1,2:T(8,128)(2,1)} %all-gather.3.cloned.1.call-done, s32[16384]{0:T(1024)S(1)} %bitcast.54, s32[512]{0:T(512)S(1)} %bitcast.56, s32[16384]{0:T(1024)S(1)} %bitcast.53, s32[512]{0:T(512)S(1)} %bitcast.55), kind=kOutput, calls=%fused_computation.12 | convolution fusion | flops 2239823872 | bytes 4460544 | tf_op jit(solution)/shard_map/dot_general | solution.py:97
  1454.5 0.7 copy.21
  1455.3 7.0 all-to-all-start.2
  1462.2 0.0 reduce-scatter.5.cloned.1.call-start
  1462.3 0.0 copy-done.1
  1462.3 1.6 broadcast_select_fusion
  1463.9 2.5 select_n.30
  1466.4 4.6 all-to-all-done.2
  1471.0 1.3 fusion.6
  1472.3 1.1 copy.24
  1473.5 0.0 reduce-scatter.5.cloned.1.call-update
  1473.5 0.0 reduce-scatter.7.cloned.1.call-start
  1473.5 32.9 %reduce-scatter.5.cloned.1.call-done = f32[128,4,128]{2,0,1:T(8,128)} async-done(((f32[512,4,128]{2,0,1:T(8,128)}), f32[128,4,128]{2,0,1:T(8,128)}) %reduce-scatter.5.cloned.1.call-update) | async-done | bytes 262160 | tf_op jit(solution)/shard_map/reduce_scatter | solution.py:46
  1506.4 0.0 reduce-scatter.7.cloned.1.call-update
  1506.5 0.0 reduce-scatter.9.cloned.1.call-start
  1506.5 26.7 %reduce-scatter.7.cloned.1.call-done = f32[32,4,128]{2,0,1:T(8,128)} async-done(((f32[128,4,128]{2,0,1:T(8,128)}), f32[32,4,128]{2,0,1:T(8,128)}) %reduce-scatter.7.cloned.1.call-update) | async-done | bytes 65552 | tf_op jit(solution)/shard_map/reduce_scatter | solution.py:46
  1533.2 0.0 reduce-scatter.9.cloned.1.call-update
  1533.2 0.0 reduce-scatter.11.cloned.1.call-start
  1533.2 26.2 %reduce-scatter.9.cloned.1.call-done = f32[16,4,128]{2,0,1:T(8,128)} async-done(((f32[32,4,128]{2,0,1:T(8,128)}), f32[16,4,128]{2,0,1:T(8,128)}) %reduce-scatter.9.cloned.1.call-update) | async-done | bytes 32784 | tf_op jit(solution)/shard_map/reduce_scatter | solution.py:46
  1559.4 0.0 reduce-scatter.11.cloned.1.call-update
  1559.4 1.3 dynamic-slice
  1560.8 12.9 reduce-scatter.11.cloned.1.call-done
  1573.7 0.7 copy.25
  1574.4 29.7 %all-reduce = f32[8,4,128]{2,1,0:T(4,128)S(1)} all-reduce(f32[8,4,128]{2,1,0:T(4,128)S(1)} %copy.25), channel_id=6, replica_groups=mesh['tm_0'=4,'tm_1'=2,'tm_2'=2,'cell_0'=8,'cell_1'=4] {'cell_0'}, use_global_device_ids=true, to_apply=%region_4.5.clone | all-reduce | flops 4096 | bytes 32768
  1604.1 1.3 dynamic-slice_bitcast_fusion
  (7 shorter events, 0.0 us)
Async XLA Ops:
  6.5 1270.1 %copy-start = (f32[16,16]{1,0:T(8,128)S(1)}, f32[16,16]{1,0:T(8,128)}, u32[]{:S(2)}) copy-start(f32[16,16]{1,0:T(8,128)} %param.8) | copy-start | bytes 3076
  6.5 1425.1 %all-gather.3.cloned.1.call-start = ((), (), s32[]{:S(2)}) async-start(), calls=%async_computation.7 | async-start | bytes 4325376 | tf_op jit(solution)/shard_map/all_gather | solution.py:95
  1145.7 131.9 %copy-start.3 = (s32[2,512]{1,0:T(2,128)S(1)}, s32[2,512]{1,0:T(2,128)}, u32[]{:S(2)}) copy-start(s32[2,512]{1,0:T(2,128)} %param.9) | copy-start | bytes 12292
  1145.7 136.4 %copy-start.2 = (s32[2048]{0:T(1024)S(1)}, s32[2048]{0:T(1024)}, u32[]{:S(2)}) copy-start(s32[2048]{0:T(1024)} %param.11) | copy-start | bytes 24580
  1278.3 17.0 %all-to-all-start = ((s32[32,2,512]{2,1,0:T(2,128)}), s32[32,2,512]{2,1,0:T(2,128)S(1)}, u32[]{:S(2)}, u32[]{:S(2)}) async-start(s32[32,2,512]{2,1,0:T(2,128)} %broadcast_in_dim.33), calls=%async_computation | async-start | bytes 262144 | tf_op jit(solution)/shard_map/all_to_all | solution.py:21
  1431.6 30.7 %copy-start.1 = (bf16[2048,512]{1,0:T(8,128)(2,1)S(1)}, bf16[2048,512]{1,0:T(8,128)(2,1)}, u32[]{:S(2)}) copy-start(bf16[2048,512]{1,0:T(8,128)(2,1)} %gather_fusion) | copy-start | bytes 6291460
  1455.3 15.8 all-to-all-start.2
  1462.2 44.2 %reduce-scatter.5.cloned.1.call-start = ((), (), s32[]{:S(2)}) async-start(), calls=%async_computation.8 | async-start | bytes 1310720 | tf_op jit(solution)/shard_map/reduce_scatter | solution.py:46
  1473.5 59.7 %reduce-scatter.7.cloned.1.call-start = ((), (), s32[]{:S(2)}) async-start(), calls=%async_computation.9 | async-start | bytes 327680 | tf_op jit(solution)/shard_map/reduce_scatter | solution.py:46
  1506.5 52.9 %reduce-scatter.9.cloned.1.call-start = ((), (), s32[]{:S(2)}) async-start(), calls=%async_computation.10 | async-start | bytes 98304 | tf_op jit(solution)/shard_map/reduce_scatter | solution.py:46
  1533.2 40.5 %reduce-scatter.11.cloned.1.call-start = ((), (), s32[]{:S(2)}) async-start(), calls=%async_computation.11 | async-start | bytes 49152 | tf_op jit(solution)/shard_map/reduce_scatter | solution.py:46
Sparse Core Ops, SparseCore 0:
  1277.7 153.8 all-gather.2
  1473.6 32.7 reduce-scatter.4
  1509.5 23.6 reduce-scatter.6
  1535.8 23.5 reduce-scatter.8
  1562.0 11.6 reduce-scatter.10
where the time goes:
time: 1610 us
  blocking collectives  1290 us (80%)
  waiting for transfers between devices  243 us (15%)
  matrix products  25.9 us (2%)
  local copies, waits for them, and re-layouts  18.6 us (1%)
    all_gather x1, blocking collectives, per_device(): lax.all_gather(duals, TM_CELL, axis=0, tiled=True)  1140 us
    all_gather x1, waiting for transfers between devices, per_device(): portion = lax.all_gather(values, CELL, axis=0, tiled=True)  136 us
    all_to_all x1, blocking collectives, per_device(): lax.all_to_all(local_adj, TM, split_axis=2, concat_axis=1, tiled=True)  126 us
    reduce_scatter x4, waiting for transfers between devices, own_block(): pieces = lax.psum_scatter(pieces, axes[k], scatter_dimension=0, tiled=True)  98.7 us
  transfers between devices with their start and end apart: 7, of which 7 were waited for; matrix products, arithmetic and copies ran while one was open for 1% of the time, Pallas kernels for 0%

commit v1 on v0

--- a/solution.py
+++ b/solution.py
@@ -8,6 +8,14 @@
 TM = ("tm_0", "tm_1", "tm_2")
 TM_CELL = ("tm_0", "tm_1", "tm_2", "cell_0", "cell_1")
 CELL = ("cell_0", "cell_1")
+
+
+def _part_task(own_rows):
+    big = jnp.concatenate(
+        lax.all_to_all(jnp.stack(jnp.split(own_rows, lax.axis_size(TM), axis=2), axis=0), TM, 0, 0),
+        axis=1,
+    )
+    return big
 
 
 def laid_out(pieces, dim):
@@ -88,7 +96,7 @@
         adjoint.astype(jnp.bfloat16).reshape(time_count, cell_count, real_count).transpose(1, 0, 2)
     )
     all_coords = gathered_copies(cell_coords, CELL, 1)
-    spread_adj = lax.all_to_all(local_adj, TM, split_axis=2, concat_axis=1, tiled=True)
+    spread_adj = _part_task(local_adj)
     values = jnp.einsum(
         "st,ctr->csr", time_cov, spread_adj.astype(jnp.float32), precision=lax.Precision.HIGHEST
     ).astype(jnp.bfloat16)

time: 1610 us -> 1610 us (level)
  no operation moved by 1% of the time
where the time goes in v1:
time: 1610 us
  blocking collectives  1290 us (80%)
  waiting for transfers between devices  243 us (15%)
  matrix products  25.6 us (2%)
  local copies, waits for them, and re-layouts  17.7 us (1%)
    all_gather x1, blocking collectives, per_device(): lax.all_gather(duals, TM_CELL, axis=0, tiled=True)  1140 us
    all_gather x1, waiting for transfers between devices, per_device(): portion = lax.all_gather(values, CELL, axis=0, tiled=True)  137 us
    all_to_all x1, blocking collectives, _part_task(): lax.all_to_all(jnp.stack(jnp.split(own_rows, lax.axis_size(TM), axis=2),...  126 us
    reduce_scatter x4, waiting for transfers between devices, own_block(): pieces = lax.psum_scatter(pieces, axes[k], scatter_dimension=0, tiled=True)  98 us
  transfers between devices with their start and end apart: 7, of which 7 were waited for; matrix products, arithmetic and copies ran while one was open for 1% of the time, Pallas kernels for 0%

profile of v1, /device:TPU:2, one launch (start us, length us, event | category | flops | bytes accessed | tf_op | source)
XLA Modules:
  0.0 1609.0 jit_solution(10315204574507560594)
XLA Ops:
  6.5 0.0 copy-start
  6.5 0.0 all-gather.3.cloned.1.call-start
  6.5 0.0 copy-start.3
  6.5 1138.5 %all-gather = bf16[512,4,128]{2,1,0:T(4,128)(2,1)S(1)} all-gather(bf16[1,4,128]{2,1,0:T(4,128)(2,1)} %bitcast.117), channel_id=1, replica_groups=mesh['tm_0'=4,'tm_1'=2,'tm_2'=2,'cell_0'=8,'cell_1'=4] {'tm_0','tm_1','t..., dimensions={0}, use_global_device_ids=true | all-gather | bytes 525312 | tf_op jit(solution)/shard_map/all_gather | solution.py:91
  1145.0 0.7 broadcast_compare_fusion
  1145.7 0.0 copy-start.2
  1145.7 1.8 select_bitcast_fusion
  1147.5 0.5 fusion.14
  1148.2 126.0 %all_to_all.19 = bf16[16,512,1,8]{1,3,2,0:T(8,128)(2,1)S(1)} all-to-all(bf16[16,512,1,8]{1,3,2,0:T(8,128)(2,1)S(1)} %constant_dynamic-update-slice_fusion), channel_id=1, replica_groups=mesh['tm_0'=4,'tm_1'=2,'tm_2'=2,'cell_0'=8,'cell_1'=4] {'tm_0','tm_1','t..., dimensions={0} | all-to-all | bytes 262144 | tf_op jit(solution)/shard_map/all_to_all | solution.py:15
  1274.2 0.0 copy-done
  1274.2 0.9 fusion.15
  1275.1 0.0 all-gather.3.cloned.1.call-update
  1275.1 0.0 copy-done.3
  1275.1 0.7 broadcast_in_dim.33
  1275.8 3.8 all-to-all-start
  1279.7 0.0 copy-done.2
  1279.7 9.2 gather_fusion
  1288.9 3.8 all-to-all-done
  1292.7 0.1 fusion.22
  1292.8 136.6 %all-gather.3.cloned.1.call-done = bf16[16384,16,8]{0,1,2:T(8,128)(2,1)} async-done(((bf16[512,16,8]{0,1,2:T(8,128)(2,1)}), bf16[16384,16,8]{0,1,2:T(8,128)(2,1)}) %all-gather.3.cloned.1.call-update) | async-done | bytes 4194320 | tf_op jit(solution)/shard_map/all_gather | solution.py:103
  1429.4 0.0 copy-start.1
  1429.4 22.9 %fusion.9 = bf16[512,16,8]{0,1,2:T(8,128)(2,1)S(1)} fusion(bf16[16384,16,8]{0,1,2:T(8,128)(2,1)} %all-gather.3.cloned.1.call-done, s32[16384]{0:T(1024)S(1)} %bitcast.114, s32[512]{0:T(512)S(1)} %bitcast.116, s32[16384]{0:T(1024)S(1)} %bitcast.113, s32[512]{0:T(512)S(1)} %bitcast.115), kind=kOutput, calls=%fused_computation.12 | convolution fusion | flops 2239823872 | bytes 4460544 | tf_op jit(solution)/shard_map/dot_general | solution.py:105
  1452.3 0.7 copy.19
  1453.1 6.9 all-to-all-start.2
  1460.0 0.0 reduce-scatter.5.cloned.1.call-start
  1460.0 0.0 copy-done.1
  1460.0 1.6 broadcast_select_fusion
  1461.6 2.5 select_n.30
  1464.2 4.6 all-to-all-done.2
  1468.8 1.3 fusion.6
  1470.1 1.1 copy.22
  1471.2 0.0 reduce-scatter.5.cloned.1.call-update
  1471.2 0.0 reduce-scatter.7.cloned.1.call-start
  1471.3 32.2 %reduce-scatter.5.cloned.1.call-done = f32[128,4,128]{2,0,1:T(8,128)} async-done(((f32[512,4,128]{2,0,1:T(8,128)}), f32[128,4,128]{2,0,1:T(8,128)}) %reduce-scatter.5.cloned.1.call-update) | async-done | bytes 262160 | tf_op jit(solution)/shard_map/reduce_scatter | solution.py:54
  1503.5 0.0 reduce-scatter.7.cloned.1.call-update
  1503.5 0.0 reduce-scatter.9.cloned.1.call-start
  1503.6 26.7 %reduce-scatter.7.cloned.1.call-done = f32[32,4,128]{2,0,1:T(8,128)} async-done(((f32[128,4,128]{2,0,1:T(8,128)}), f32[32,4,128]{2,0,1:T(8,128)}) %reduce-scatter.7.cloned.1.call-update) | async-done | bytes 65552 | tf_op jit(solution)/shard_map/reduce_scatter | solution.py:54
  1530.3 0.0 reduce-scatter.9.cloned.1.call-update
  1530.3 0.0 reduce-scatter.11.cloned.1.call-start
  1530.3 26.2 %reduce-scatter.9.cloned.1.call-done = f32[16,4,128]{2,0,1:T(8,128)} async-done(((f32[32,4,128]{2,0,1:T(8,128)}), f32[16,4,128]{2,0,1:T(8,128)}) %reduce-scatter.9.cloned.1.call-update) | async-done | bytes 32784 | tf_op jit(solution)/shard_map/reduce_scatter | solution.py:54
  1556.5 0.0 reduce-scatter.11.cloned.1.call-update
  1556.5 1.3 dynamic-slice
  1557.9 12.9 reduce-scatter.11.cloned.1.call-done
  1570.8 0.7 copy.23
  1571.5 29.7 %all-reduce = f32[8,4,128]{2,1,0:T(4,128)S(1)} all-reduce(f32[8,4,128]{2,1,0:T(4,128)S(1)} %copy.23), channel_id=6, replica_groups=mesh['tm_0'=4,'tm_1'=2,'tm_2'=2,'cell_0'=8,'cell_1'=4] {'cell_0'}, use_global_device_ids=true, to_apply=%region_4.5.clone | all-reduce | flops 4096 | bytes 32768
  1601.2 1.2 dynamic-slice_bitcast_fusion
  (19 shorter events, 0.1 us)
Async XLA Ops:
  6.5 1267.7 %copy-start = (f32[16,16]{1,0:T(8,128)S(1)}, f32[16,16]{1,0:T(8,128)}, u32[]{:S(2)}) copy-start(f32[16,16]{1,0:T(8,128)} %param.8) | copy-start | bytes 3076
  6.5 1422.9 %all-gather.3.cloned.1.call-start = ((), (), s32[]{:S(2)}) async-start(), calls=%async_computation.7 | async-start | bytes 4325376 | tf_op jit(solution)/shard_map/all_gather | solution.py:103
  6.5 1268.6 %copy-start.3 = (s32[2,512]{1,0:T(2,128)S(1)}, s32[2,512]{1,0:T(2,128)}, u32[]{:S(2)}) copy-start(s32[2,512]{1,0:T(2,128)} %param.9) | copy-start | bytes 12292
  1145.7 133.9 %copy-start.2 = (s32[2048]{0:T(1024)S(1)}, s32[2048]{0:T(1024)}, u32[]{:S(2)}) copy-start(s32[2048]{0:T(1024)} %param.11) | copy-start | bytes 24580
  1275.8 16.9 %all-to-all-start = ((s32[32,2,512]{2,1,0:T(2,128)}), s32[32,2,512]{2,1,0:T(2,128)S(1)}, u32[]{:S(2)}, u32[]{:S(2)}) async-start(s32[32,2,512]{2,1,0:T(2,128)} %broadcast_in_dim.33), calls=%async_computation | async-start | bytes 262144 | tf_op jit(solution)/shard_map/all_to_all | solution.py:29
  1429.4 30.6 %copy-start.1 = (bf16[2048,512]{1,0:T(8,128)(2,1)S(1)}, bf16[2048,512]{1,0:T(8,128)(2,1)}, u32[]{:S(2)}) copy-start(bf16[2048,512]{1,0:T(8,128)(2,1)} %gather_fusion) | copy-start | bytes 6291460
  1453.1 15.7 all-to-all-start.2
  1460.0 43.5 %reduce-scatter.5.cloned.1.call-start = ((), (), s32[]{:S(2)}) async-start(), calls=%async_computation.8 | async-start | bytes 1310720 | tf_op jit(solution)/shard_map/reduce_scatter | solution.py:54
  1471.2 59.0 %reduce-scatter.7.cloned.1.call-start = ((), (), s32[]{:S(2)}) async-start(), calls=%async_computation.9 | async-start | bytes 327680 | tf_op jit(solution)/shard_map/reduce_scatter | solution.py:54
  1503.5 53.0 %reduce-scatter.9.cloned.1.call-start = ((), (), s32[]{:S(2)}) async-start(), calls=%async_computation.10 | async-start | bytes 98304 | tf_op jit(solution)/shard_map/reduce_scatter | solution.py:54
  1530.3 40.5 %reduce-scatter.11.cloned.1.call-start = ((), (), s32[]{:S(2)}) async-start(), calls=%async_computation.11 | async-start | bytes 49152 | tf_op jit(solution)/shard_map/reduce_scatter | solution.py:54
Sparse Core Ops, SparseCore 0:
  1275.2 154.1 all-gather.2
  1471.4 32.1 reduce-scatter.4
  1506.6 23.6 reduce-scatter.6
  1532.8 23.6 reduce-scatter.8
  1559.1 11.6 reduce-scatter.10
